TPU v7x, 32 devices: a whole 2x2x4 slice. The times are simulated.
32 devices in a mesh: parts: 2 (over y), row: 8 (over z, x), col: 2 (over core).
Axes of the slice: x: 2, y: 2, z: 4, core: 2. Of those that a mesh axis runs over, the one named last changes fastest.
Arguments:
- amplitudes: bfloat16 [16, 2, 2048, 256], P(('parts', 'row'), 'col'), parts along dimension 0, may hold values from -6 to 6
- integrals: bfloat16 [4, 2048, 2, 256], P(('parts', 'col')), parts along dimension 0, may hold values from -0.25 to 0.25
- orbital_irrep: int32 [16], P('parts'), parts along dimension 0, may hold values from 0 to 7, as said below
- slab_irrep: int32 [8], P('parts'), parts along dimension 0, may hold values from 0 to 7
- virtual_count: int32 [16], P('parts'), parts along dimension 0, may hold values from 128 to 256, as said below
Outputs:
- residual: bfloat16 [16, 2, 2048, 256], P('parts', 'col', 'row'), parts along dimension 0
There are 2 independent parts, one for each index of `parts`. A program takes and returns all parts, laid end to end along the dimension named above; each array names one. Nothing has to cross between parts.
Inputs may be any that keep to these rules, and one draw needn't show every extreme that they name: orbital_irrep never falls along the orbitals i; each irrep labels at most 2 of them, and some irrep exactly 2. `virtual_count`: some irrep has all 256 places real.
All inputs are finite; a program needn't handle non-finite values.
Results may differ from a plain program's by a relative error of at most 0.001.
Values may be sent and summed in bfloat16 or wider, within the bound.
A program may use at most 64 MiB of HBM per device.

v0:
```python
import jax
import jax.numpy as jnp
from jax import lax
from jax.sharding import PartitionSpec as P


def label_lookup(table, labels):
    symmetries = jnp.arange(table.shape[0], dtype=jnp.int32)
    return jnp.sum(jnp.where(labels[..., None] == symmetries, table, 0), axis=-1)


def masked_tiles(integrals, pair_labels, column_labels, virtual_count):
    slab_count, virtual_total, column_count, width = integrals.shape
    group_total = virtual_count.shape[0]
    integral_tiles = integrals.reshape(slab_count, group_total, width, column_count, width)
    symmetries = jnp.arange(group_total, dtype=jnp.int32)
    places = jnp.arange(width, dtype=jnp.int32)
    inner_keep = places[None, :] < virtual_count[:, None]
    outer_block = (
        symmetries[None, :, None] ^ pair_labels[:, None, None] ^ column_labels[None, None, :]
    )
    outer_keep = places < label_lookup(virtual_count, outer_block)[..., None]
    keep_mask = inner_keep[None, :, :, None, None] & outer_keep[:, :, None, :, :]
    return jnp.where(keep_mask, integral_tiles, jnp.zeros((), integrals.dtype))


def contract_rows(source_block, integral_tiles, row_labels, pair_labels, virtual_label):
    occupied = source_block.shape[0]
    group_rows = occupied // 4
    group_total = integral_tiles.shape[1]
    symmetries = jnp.arange(group_total, dtype=jnp.int32)
    padded = jnp.concatenate(
        [source_block, jnp.zeros((group_rows,) + source_block.shape[1:], source_block.dtype)],
        axis=0,
    )
    group_sizes = jnp.sum((row_labels[:, None] == symmetries[None, :]).astype(jnp.int32), axis=0)
    group_starts = jnp.cumsum(group_sizes) - group_sizes
    collected = jnp.zeros(
        (
            occupied + group_rows,
            integral_tiles.shape[3],
            source_block.shape[2],
            source_block.shape[3],
        ),
        jnp.float32,
    )
    slab_index = jnp.arange(integral_tiles.shape[0], dtype=jnp.int32)
    row_number = jnp.arange(group_rows, dtype=jnp.int32)
    for symmetry in range(group_total):
        first_row = group_starts[symmetry]
        row_block = lax.dynamic_slice_in_dim(padded, first_row, group_rows, 0)
        selected = integral_tiles[slab_index, virtual_label ^ symmetry ^ pair_labels]
        partial_block = jnp.einsum(
            "ikac,kcjb->ijab", row_block, selected, preferred_element_type=jnp.float32
        )
        in_group = row_number < group_sizes[symmetry]
        previous = lax.dynamic_slice_in_dim(collected, first_row, group_rows, 0)
        merged = jnp.where(in_group[:, None, None, None], partial_block, previous)
        collected = lax.dynamic_update_slice_in_dim(collected, merged, first_row, 0)
    return collected[:occupied]


def mask_rows(values, first_virtual, virtual_count):
    width = values.shape[3]
    virtual_index = first_virtual + jnp.arange(values.shape[2], dtype=jnp.int32)
    real_place = virtual_index % width < label_lookup(virtual_count, virtual_index // width)
    return jnp.where(real_place[None, None, :, None], values, 0.0)


def reduce_halves(partial_sums):
    return lax.psum_scatter(partial_sums, "col", scatter_dimension=1, tiled=True)


def per_device(amplitudes, integrals, orbital_irrep, slab_irrep, virtual_count):
    half_slab = amplitudes.shape[1]
    block_width = integrals.shape[3]
    col_place = lax.axis_index("col")
    row_place = lax.axis_index("row")
    own_pairs = lax.dynamic_slice_in_dim(slab_irrep, col_place * half_slab, half_slab)
    column_labels = slab_irrep[2 * half_slab :]
    integral_tiles = masked_tiles(integrals, own_pairs, column_labels, virtual_count)
    spread = lax.all_to_all(amplitudes, "row", split_axis=2, concat_axis=0, tiled=True)
    spread_width = spread.shape[2]
    first_virtual = row_place * spread_width
    virtual_label = first_virtual // block_width
    summed = reduce_halves(
        contract_rows(spread, integral_tiles, orbital_irrep, own_pairs, virtual_label)
    )
    return mask_rows(summed, first_virtual, virtual_count).astype(jnp.bfloat16)


def solution(mesh):
    in_specs = (
        P(("parts", "row"), "col", None, None),
        P(("parts", "col"), None, None, None),
        P("parts"),
        P("parts"),
        P("parts"),
    )
    out_specs = P("parts", "col", "row", None)
    return jax.shard_map(
        per_device, mesh=mesh, in_specs=in_specs, out_specs=out_specs, check_vma=False
    )
```

profile of v0, /device:TPU:9, one launch (start us, length us, event | category | flops | bytes accessed | tf_op | source)
XLA Modules:
  0.0 98.2 jit_solution(2858224833565637630)
XLA Ops:
  6.5 3.2 %copy.28 = bf16[1,1,2048,256]{3,1,0,2:T(2,128)(2,1)S(1)} copy(bf16[1,1,2048,256]{3,2,1,0:T(8,128)(2,1)} %param.5) | data formatting | bytes 2097152 | tf_op args[0]
  9.7 0.5 broadcast.377
  10.2 10.6 %reduce.1 = bf16[2048,256]{1,0:T(8,128)(2,1)S(1)} reduce(bf16[2048,1,1,256]{3,2,1,0:T(2,128)(2,1)S(1)} %bitcast.185, bf16[]{:T(256)} %broadcast.377), dimensions={1,2}, to_apply=%bitcast.175.reduce_sub_computation | reduce | bytes 2097154
  20.8 0.0 copy-start.2
  20.8 0.0 copy-start.3
  20.9 0.0 copy-start.1
  20.9 0.0 copy-start
  20.9 1.1 %reshape.523 = bf16[8,2,32768]{2,1,0:T(2,128)(2,1)} reshape(bf16[2048,256]{1,0:T(8,128)(2,1)S(1)} %reduce.1) | data formatting | bytes 2097152
  22.0 5.7 %all-to-all-start = ((bf16[8,2,32768]{2,1,0:T(2,128)(2,1)}), bf16[8,2,32768]{2,1,0:T(2,128)(2,1)S(1)}, u32[]{:S(2)}, u32[]{:S(2)}) async-start(bf16[8,2,32768]{2,1,0:T(2,128)(2,1)} %reshape.523), calls=%async_computation | async-start | bytes 2097152 | tf_op jit(solution)/shard_map/all_to_all | solution.py:82
  27.7 0.0 reduce-scatter.2.cloned.1.call-start
  27.7 0.0 copy-done.2
  27.7 0.1 slice.55
  27.8 0.7 dynamic_slice.51
  28.4 0.0 copy-done.3
  28.4 0.1 convert_reduce_fusion
  28.5 0.2 reduce-window.9
  28.7 0.7 iota_xor_fusion
  29.4 0.1 broadcast_xor_fusion
  29.5 0.0 copy-done.1
  29.5 0.2 select_reduce_fusion
  29.7 0.7 fusion.67
  45.8 0.1 copy.14
  45.9 0.0 copy-done
  45.9 3.7 %copy.15 = bf16[1,8,256,2,256]{2,4,3,1,0:T(8,128)(2,1)} copy(bf16[1,8,256,2,256]{4,3,2,1,0:T(2,128)(2,1)S(1)} %bitcast.186) | data formatting | bytes 4194304 | tf_op jit(solution)/shard_map/reshape | solution.py:15
  54.6 0.7 fusion.66
  55.3 0.6 iota_compare_fusion.12
  55.9 0.6 iota_compare_fusion.11
  56.5 0.6 iota_compare_fusion.10
  57.1 0.7 iota_compare_fusion.9
  57.8 0.7 iota_compare_fusion.8
  58.4 0.6 iota_compare_fusion.7
  59.1 0.6 iota_compare_fusion.6
  59.7 0.6 iota_compare_fusion.5
  60.3 0.1 iota_compare_fusion.2
  60.4 0.1 iota_compare_fusion
  60.5 2.1 %and_select_fusion = bf16[1,8,256,2,256]{2,4,3,1,0:T(8,128)(2,1)S(1)} fusion(bf16[1,8,256,2,256]{2,4,3,1,0:T(8,128)(2,1)} %copy.15, pred[8,2,256]{2,1,0:T(4,128)(4,1)S(1)} %iota_compare_fusion, pred[8,256]{1,0:T(8,128)(4,1)S(1)} %iota_compare_fusion.2), kind=kLoop, calls=%fused_computation | loop fusion | flops 2097152 | bytes 4200448 | tf_op jit(solution)/shard_map/jit(_where)/select_n | solution.py:24
  62.6 0.0 all-to-all-done
  62.6 3.5 %reshape.524 = bf16[2048,1,1,256]{3,2,1,0:T(2,128)(2,1)} reshape(bf16[8,2,32768]{2,1,0:T(2,128)(2,1)S(1)} %all-to-all-done) | data formatting | bytes 2097152
  66.1 1.8 %copy.26 = bf16[1,1,2048,256]{3,2,0,1:T(8,128)(2,1)S(1)} copy(bf16[1,1,2048,256]{3,1,0,2:T(2,128)(2,1)} %bitcast.184) | data formatting | bytes 2097152
  67.8 0.5 broadcast_in_dim.130
  68.4 0.4 fusion.15
  68.7 0.4 fusion.1
  69.1 0.4 fusion.3
  69.5 0.4 fusion.5
  69.9 0.4 fusion.7
  70.3 0.4 fusion.9
  70.7 0.4 fusion.11
  71.1 0.4 fusion.13
  71.5 2.4 %slice.200 = f32[8,2,256,256]{2,3,0,1:T(8,128)} slice(f32[10,2,256,256]{2,3,0,1:T(8,128)S(1)} %fusion.13), slice={[0:8], [0:2], [0:256], [0:256]} | slice | bytes 8388608 | tf_op jit(solution)/shard_map/slice | solution.py:60
  73.8 0.0 reduce-scatter.2.cloned.1.call-update
  73.9 0.1 select_reduce_fusion.1
  74.0 14.3 %reduce-scatter.2.cloned.1.call-done = f32[8,1,256,256]{2,3,0,1:T(8,128)} async-done(((f32[8,2,256,256]{2,3,0,1:T(8,128)}), f32[8,1,256,256]{2,3,0,1:T(8,128)}) %reduce-scatter.2.cloned.1.call-update) | async-done | bytes 2097168 | tf_op jit(solution)/shard_map/reduce_scatter | solution.py:71
  88.3 1.8 %select_convert_fusion = bf16[8,1,256,256]{2,3,0,1:T(8,128)(2,1)S(1)} fusion(f32[8,1,256,256]{2,3,0,1:T(8,128)} %reduce-scatter.2.cloned.1.call-done, pred[256]{0:T(512)(128)(4,1)S(1)} %fusion.56), kind=kLoop, calls=%fused_computation.1 | loop fusion | flops 524288 | bytes 3145984 | tf_op jit(solution)/shard_map/convert_element_type | solution.py:89
  90.0 1.3 %copy.17 = bf16[8,1,256,256]{3,2,1,0:T(8,128)(2,1)} copy(bf16[8,1,256,256]{2,3,0,1:T(8,128)(2,1)S(1)} %select_convert_fusion) | data formatting | bytes 2097152 | tf_op jit(solution)/shard_map/convert_element_type | solution.py:89
  (3 shorter events, 0.0 us)
Async XLA Ops:
  20.8 6.8 %copy-start.2 = (s32[4]{0:T(128)S(1)}, s32[4]{0:T(128)}, u32[]{:S(2)}) copy-start(s32[4]{0:T(128)} %param.8) | copy-start | bytes 52
  20.8 7.6 %copy-start.3 = (s32[8]{0:T(128)S(1)}, s32[8]{0:T(128)}, u32[]{:S(2)}) copy-start(s32[8]{0:T(128)} %param.7) | copy-start | bytes 100
  20.9 8.6 %copy-start.1 = (s32[8]{0:T(128)S(1)}, s32[8]{0:T(128)}, u32[]{:S(2)}) copy-start(s32[8]{0:T(128)} %param.9) | copy-start | bytes 100
  20.9 25.0 %copy-start = (bf16[1,2048,2,256]{3,2,1,0:T(2,128)(2,1)S(1)}, bf16[1,2048,2,256]{3,2,1,0:T(2,128)(2,1)}, u32[]{:S(2)}) copy-start(bf16[1,2048,2,256]{3,2,1,0:T(2,128)(2,1)} %param.6) | copy-start | bytes 6291460
  22.0 40.6 %all-to-all-start = ((bf16[8,2,32768]{2,1,0:T(2,128)(2,1)}), bf16[8,2,32768]{2,1,0:T(2,128)(2,1)S(1)}, u32[]{:S(2)}, u32[]{:S(2)}) async-start(bf16[8,2,32768]{2,1,0:T(2,128)(2,1)} %reshape.523), calls=%async_computation | async-start | bytes 2097152 | tf_op jit(solution)/shard_map/all_to_all | solution.py:82
  27.7 60.6 %reduce-scatter.2.cloned.1.call-start = ((), (), s32[]{:S(2)}) async-start(), calls=%async_computation.2 | async-start | bytes 6291456 | tf_op jit(solution)/shard_map/reduce_scatter | solution.py:71
Sparse Core Ops, SparseCore 0:
  74.0 14.2 reduce-scatter.1
where the time goes:
time: 99.7 us; the launch traced here: 98.2 us
  between operations  34 us (34%)
  other arithmetic  21 us (21%)
  local copies, waits for them, and re-layouts  20.2 us (20%)
  waiting for transfers between devices  14.3 us (14%)
  starting transfers between devices  5.69 us (6%)
  matrix products  3.07 us (3%)
    reduce_scatter x1, waiting for transfers between devices, reduce_halves(): lax.psum_scatter(partial_sums, 'col', scatter_dimension=1, tiled=True)  14.3 us
    unnamed x1, other arithmetic  10.6 us
    unnamed x13, local copies, waits for them, and re-layouts  10 us
    all_to_all x1, starting transfers between devices, per_device(): lax.all_to_all(amplitudes, 'row', split_axis=2, concat_axis=0, tiled=True)  5.69 us
    lt x8, other arithmetic, contract_rows(): in_group = row_number < group_sizes[symmetry]  5.02 us
    reshape x1, local copies, waits for them, and re-layouts, masked_tiles(): integrals.reshape(slab_count, group_total, width, column_count, width)  3.74 us
    dot_general x8, matrix products, contract_rows(): jnp.einsum('ikac,kcjb->ijab', row_block, selected, preferred_element_type...  3.07 us
    slice x1, local copies, waits for them, and re-layouts, contract_rows(): return collected[:occupied]  2.36 us
  transfers between devices with their start and end apart: 2, of which 1 were waited for; matrix products, arithmetic and copies ran while one was open for 15% of the time, Pallas kernels for 0%

commit v1 on v0

v1 whole, which is shorter than its diff:
```python
import functools

import jax
import jax.numpy as jnp
from jax import lax
from jax.experimental import pallas as pl
from jax.experimental.pallas import tpu as pltpu
from jax.sharding import PartitionSpec as P

MESH = pl.DeviceIdType.MESH


def partner_of(me, step, count):
    if count & (count - 1):
        return (me + step) % count
    place, bit = 0, 1
    while bit < count:
        place = place + (((me // bit) % 2 + (step // bit) % 2) % 2) * bit
        bit *= 2
    return place


def each(low, high, body):
    if high - low <= 16:
        for step in range(low, high):
            body(step)
    else:
        lax.fori_loop(low, high, lambda step, carry: (body(step), carry)[1], 0)


def kernel(
    count,
    label_ref, slab_ref, size_ref, amp_ref, int_ref, out_ref,
    landed, shared, staged, raw, own_tiles, sent_tiles, other_tiles,
    send_sem, land_sem, pass_sem, share_sem, out_sem, raw_sem, tile_sem, own_sem,
):
    me = lax.axis_index("row")
    col = lax.axis_index("col")
    sibling = 1 - col
    rows = landed.shape[1]
    width = landed.shape[2]
    groups = own_tiles.shape[0]

    raw_copies = [
        pltpu.make_async_copy(
            int_ref.at[0, pl.ds(e * width, width)], raw.at[e], raw_sem.at[e]
        )
        for e in range(groups)
    ]
    own_copy = pltpu.make_async_copy(
        amp_ref.at[0, 0, pl.ds(pl.multiple_of(me * rows, rows), rows)], landed.at[me], own_sem
    )

    barrier = pltpu.get_barrier_semaphore()

    def greet(step):
        pl.semaphore_signal(
            barrier, inc=1, device_id={"row": partner_of(me, step, count)}, device_id_type=MESH
        )

    each(1, count, greet)
    pl.semaphore_signal(barrier, inc=1, device_id={"col": sibling}, device_id_type=MESH)
    pl.semaphore_wait(barrier, count)

    def spread_copy(step):
        there = partner_of(me, step, count)
        return pltpu.make_async_remote_copy(
            src_ref=amp_ref.at[0, 0, pl.ds(pl.multiple_of(there * rows, rows), rows)],
            dst_ref=landed.at[me],
            send_sem=send_sem.at[step],
            recv_sem=land_sem.at[step],
            device_id={"row": there},
            device_id_type=MESH,
        )

    each(1, count, lambda step: spread_copy(count - step).start())
    own_copy.start()
    for copy in raw_copies:
        copy.start()

    own_label = slab_ref[col]
    place = lax.broadcasted_iota(jnp.int32, (width, width), 0)
    column = lax.broadcasted_iota(jnp.int32, (width, width), 1)

    def keep(tile, e, j):
        outer = size_ref[e ^ own_label ^ slab_ref[2 + j]]
        return jnp.where((place < size_ref[e]) & (column < outer), tile, jnp.zeros((), tile.dtype))

    tile_copies = []
    for e in range(groups):
        raw_copies[e].wait()
        tile_pair = raw[e]
        first = tile_pair[:, 0, :]
        second = tile_pair[:, 1, :]
        mine = jnp.where(col == 0, first, second)
        other = jnp.where(col == 0, second, first)
        sent_tiles[e] = keep(other, e, sibling)
        copy = pltpu.make_async_remote_copy(
            src_ref=sent_tiles.at[e],
            dst_ref=other_tiles.at[e],
            send_sem=tile_sem.at[0, e],
            recv_sem=tile_sem.at[1, e],
            device_id={"col": sibling},
            device_id_type=MESH,
        )
        copy.start()
        tile_copies.append(copy)
        own_tiles[e] = keep(mine, e, col)

    def share_copy(step):
        source = partner_of(me, step, count)
        return pltpu.make_async_remote_copy(
            src_ref=landed.at[source],
            dst_ref=shared.at[source],
            send_sem=pass_sem.at[step],
            recv_sem=share_sem.at[step],
            device_id={"col": sibling},
            device_id_type=MESH,
        )

    first_virtual = me * rows
    group = first_virtual // width
    offset = first_virtual % width
    row_place = lax.broadcasted_iota(jnp.int32, (rows, width), 0) + offset
    row_keep = row_place < size_ref[group]
    other_label = slab_ref[sibling]

    def out_copy(step):
        source = partner_of(me, step, count)
        return pltpu.make_async_copy(staged.at[source], out_ref.at[source, 0], out_sem.at[step])

    def finish(step):
        source = partner_of(me, step, count)
        share_copy(step).wait_recv()
        label = group ^ label_ref[source]
        total = jnp.dot(
            landed[source], own_tiles[label ^ own_label], preferred_element_type=jnp.float32
        )
        total = total + jnp.dot(
            shared[source], other_tiles[label ^ other_label], preferred_element_type=jnp.float32
        )
        staged[source] = jnp.where(row_keep, total, 0.0).astype(staged.dtype)
        out_copy(step).start()

    own_copy.wait()
    share_copy(0).start()
    for copy in tile_copies:
        copy.wait_recv()

    def arrive(step):
        spread_copy(step).wait_recv()
        share_copy(step).start()
        finish(step - 1)

    each(1, count, arrive)
    finish(count - 1)

    for copy in tile_copies:
        copy.wait_send()
    each(1, count, lambda step: spread_copy(step).wait_send())
    each(0, count, lambda step: share_copy(step).wait_send())
    each(0, count, lambda step: out_copy(step).wait())


def per_device(amplitudes, integrals, orbital_irrep, slab_irrep, virtual_count, count):
    virtual_total, width = amplitudes.shape[2:]
    groups = virtual_count.shape[0]
    rows = virtual_total // count
    kind = amplitudes.dtype
    smem = pl.BlockSpec(memory_space=pltpu.SMEM)
    anywhere = pl.BlockSpec(memory_space=pl.ANY)
    dma = pltpu.SemaphoreType.DMA
    return pl.pallas_call(
        functools.partial(kernel, count),
        out_shape=jax.ShapeDtypeStruct((count, 1, rows, width), kind),
        in_specs=[smem, smem, smem, anywhere, anywhere],
        out_specs=anywhere,
        scratch_shapes=[
            pltpu.VMEM((count, rows, width), kind),
            pltpu.VMEM((count, rows, width), kind),
            pltpu.VMEM((count, rows, width), kind),
            pltpu.VMEM((groups, width, 2, width), kind),
            pltpu.VMEM((groups, width, width), kind),
            pltpu.VMEM((groups, width, width), kind),
            pltpu.VMEM((groups, width, width), kind),
            dma((count,)),
            dma((count,)),
            dma((count,)),
            dma((count,)),
            dma((count,)),
            dma((groups,)),
            dma((2, groups)),
            dma,
        ],
        compiler_params=pltpu.CompilerParams(
            collective_id=0, has_side_effects=True, vmem_limit_bytes=48 * 1024 * 1024
        ),
    )(orbital_irrep, slab_irrep, virtual_count, amplitudes, integrals)


def solution(mesh):
    in_specs = (
        P(("parts", "row"), "col", None, None),
        P(("parts", "col"), None, None, None),
        P("parts"),
        P("parts"),
        P("parts"),
    )
    return jax.shard_map(
        functools.partial(per_device, count=mesh.shape["row"]),
        mesh=mesh,
        in_specs=in_specs,
        out_specs=P("parts", "col", "row", None),
        check_vma=False,
    )
```

time: 99.7 us -> 40.4 us (0.41)
  the two profiles are of different devices: /device:TPU:9 before, /device:TPU:0 now
where the time goes in v1:
time: 40.4 us; the launch traced here: 40.2 us
  Pallas kernels  34.4 us (85%)
  local copies, waits for them, and re-layouts  5.75 us (14%)
    pallas_call x1, Pallas kernels, per_device(): pl.pallas_call(functools.partial(kernel, count), out_shape=jax.ShapeDtype...  34.4 us
    unnamed x11, local copies, waits for them, and re-layouts  5.75 us

profile of v1, /device:TPU:0, one launch (start us, length us, event | category | flops | bytes accessed | tf_op | source)
XLA Modules:
  0.0 40.2 jit_solution(16070673479872395046)
XLA Ops:
  0.0 0.0 copy-start
  0.0 1.6 %copy-done = bf16[1,2048,2,256]{3,2,1,0:T(2,128)(2,1)S(1)} copy-done((bf16[1,2048,2,256]{3,2,1,0:T(2,128)(2,1)S(1)}, bf16[1,2048,2,256]{3,2,1,0:T(2,128)(2,1)}, u32[]{:S(2)}) %copy-start) | copy-done | bytes 2097176
  1.6 0.0 copy-start.1
  1.6 1.2 %copy-done.1 = bf16[1,1,2048,256]{3,2,1,0:T(8,128)(2,1)S(1)} copy-done((bf16[1,1,2048,256]{3,2,1,0:T(8,128)(2,1)S(1)}, bf16[1,1,2048,256]{3,2,1,0:T(8,128)(2,1)}, u32[]{:S(2)}) %copy-start.1) | copy-done | bytes 1048600
  2.8 0.0 copy-start.2
  2.8 0.7 %copy-done.2 = s32[8]{0:T(128)S(1)} copy-done((s32[8]{0:T(128)S(1)}, s32[8]{0:T(128)}, u32[]{:S(2)}) %copy-start.2) | copy-done | bytes 56
  3.5 0.0 copy-start.3
  3.5 0.7 %copy-done.3 = s32[4]{0:T(128)S(1)} copy-done((s32[4]{0:T(128)S(1)}, s32[4]{0:T(128)}, u32[]{:S(2)}) %copy-start.3) | copy-done | bytes 40
  4.1 0.0 copy-start.4
  4.1 0.7 %copy-done.4 = s32[8]{0:T(128)S(1)} copy-done((s32[8]{0:T(128)S(1)}, s32[8]{0:T(128)}, u32[]{:S(2)}) %copy-start.4) | copy-done | bytes 56
  4.8 34.4 %shard_map.55 = bf16[8,1,256,256]{3,2,1,0:T(8,128)(2,1)S(1)} custom-call(s32[8]{0:T(128)S(1)} %copy-done.2, s32[4]{0:T(128)S(1)} %copy-done.3, s32[8]{0:T(128)S(1)} %copy-done.4, bf16[1,1,2048,256]{3,2,1,0:T(8,128)(2,1)S(1)} %copy-done.1, bf16[1,2048,2,256]{3,2,1,0:T(2,128)(2,1)S(1)} %copy-done), custom_call_target="tpu_custom_call" | custom-call | tf_op jit(solution)/shard_map/pallas_call | solution.py:173
  39.2 1.0 %copy.7 = bf16[8,1,256,256]{3,2,1,0:T(8,128)(2,1)} copy(bf16[8,1,256,256]{3,2,1,0:T(8,128)(2,1)S(1)} %shard_map.55) | data formatting | bytes 2097152
Async XLA Ops:
  0.0 1.6 %copy-start = (bf16[1,2048,2,256]{3,2,1,0:T(2,128)(2,1)S(1)}, bf16[1,2048,2,256]{3,2,1,0:T(2,128)(2,1)}, u32[]{:S(2)}) copy-start(bf16[1,2048,2,256]{3,2,1,0:T(2,128)(2,1)} %int_ref.1) | copy-start | bytes 6291460
  1.6 1.2 %copy-start.1 = (bf16[1,1,2048,256]{3,2,1,0:T(8,128)(2,1)S(1)}, bf16[1,1,2048,256]{3,2,1,0:T(8,128)(2,1)}, u32[]{:S(2)}) copy-start(bf16[1,1,2048,256]{3,2,1,0:T(8,128)(2,1)} %amp_ref.1) | copy-start | bytes 3145732
  2.8 0.7 %copy-start.2 = (s32[8]{0:T(128)S(1)}, s32[8]{0:T(128)}, u32[]{:S(2)}) copy-start(s32[8]{0:T(128)} %label_ref.1) | copy-start | bytes 100
  3.5 0.7 %copy-start.3 = (s32[4]{0:T(128)S(1)}, s32[4]{0:T(128)}, u32[]{:S(2)}) copy-start(s32[4]{0:T(128)} %slab_ref.1) | copy-start | bytes 52
  4.1 0.7 %copy-start.4 = (s32[8]{0:T(128)S(1)}, s32[8]{0:T(128)}, u32[]{:S(2)}) copy-start(s32[8]{0:T(128)} %size_ref.1) | copy-start | bytes 100

commit v2 on v1

--- a/solution.py
+++ b/solution.py
@@ -10,9 +10,9 @@
 MESH = pl.DeviceIdType.MESH
 
 
-def partner_of(me, step, count):
+def partner_of(me, step, count, back=False):
     if count & (count - 1):
-        return (me + step) % count
+        return (me + (count - step if back else step)) % count
     place, bit = 0, 1
     while bit < count:
         place = place + (((me // bit) % 2 + (step // bit) % 2) % 2) * bit
@@ -30,9 +30,9 @@
 
 def kernel(
     count,
-    label_ref, slab_ref, size_ref, amp_ref, int_ref, out_ref,
-    landed, shared, staged, raw, own_tiles, sent_tiles, other_tiles,
-    send_sem, land_sem, pass_sem, share_sem, out_sem, raw_sem, tile_sem, own_sem,
+    label_hbm, slab_hbm, size_hbm, amp_ref, int_ref, out_ref,
+    label_ref, slab_ref, size_ref, landed, shared, staged, raw, own_tiles, sent_tiles, other_tiles,
+    send_sem, land_sem, pass_sem, share_sem, out_sem, raw_sem, tile_sem, own_sem, label_sem,
 ):
     me = lax.axis_index("row")
     col = lax.axis_index("col")
@@ -50,6 +50,16 @@
     own_copy = pltpu.make_async_copy(
         amp_ref.at[0, 0, pl.ds(pl.multiple_of(me * rows, rows), rows)], landed.at[me], own_sem
     )
+
+    label_copies = [
+        pltpu.make_async_copy(source, place, label_sem.at[number])
+        for number, (source, place) in enumerate(
+            [(label_hbm, label_ref), (slab_hbm, slab_ref), (size_hbm, size_ref)]
+        )
+    ]
+    for copy in label_copies + raw_copies:
+        copy.start()
+    own_copy.start()
 
     barrier = pltpu.get_barrier_semaphore()
 
@@ -73,10 +83,9 @@
             device_id_type=MESH,
         )
 
-    each(1, count, lambda step: spread_copy(count - step).start())
-    own_copy.start()
-    for copy in raw_copies:
-        copy.start()
+    each(1, count, lambda step: spread_copy(step).start())
+    for copy in label_copies:
+        copy.wait()
 
     own_label = slab_ref[col]
     place = lax.broadcasted_iota(jnp.int32, (width, width), 0)
@@ -108,7 +117,7 @@
         own_tiles[e] = keep(mine, e, col)
 
     def share_copy(step):
-        source = partner_of(me, step, count)
+        source = partner_of(me, step, count, back=True)
         return pltpu.make_async_remote_copy(
             src_ref=landed.at[source],
             dst_ref=shared.at[source],
@@ -126,11 +135,11 @@
     other_label = slab_ref[sibling]
 
     def out_copy(step):
-        source = partner_of(me, step, count)
+        source = partner_of(me, step, count, back=True)
         return pltpu.make_async_copy(staged.at[source], out_ref.at[source, 0], out_sem.at[step])
 
     def finish(step):
-        source = partner_of(me, step, count)
+        source = partner_of(me, step, count, back=True)
         share_copy(step).wait_recv()
         label = group ^ label_ref[source]
         total = jnp.dot(
@@ -167,15 +176,17 @@
     groups = virtual_count.shape[0]
     rows = virtual_total // count
     kind = amplitudes.dtype
-    smem = pl.BlockSpec(memory_space=pltpu.SMEM)
     anywhere = pl.BlockSpec(memory_space=pl.ANY)
     dma = pltpu.SemaphoreType.DMA
     return pl.pallas_call(
         functools.partial(kernel, count),
         out_shape=jax.ShapeDtypeStruct((count, 1, rows, width), kind),
-        in_specs=[smem, smem, smem, anywhere, anywhere],
+        in_specs=[anywhere] * 5,
         out_specs=anywhere,
         scratch_shapes=[
+            pltpu.SMEM(orbital_irrep.shape, jnp.int32),
+            pltpu.SMEM(slab_irrep.shape, jnp.int32),
+            pltpu.SMEM(virtual_count.shape, jnp.int32),
             pltpu.VMEM((count, rows, width), kind),
             pltpu.VMEM((count, rows, width), kind),
             pltpu.VMEM((count, rows, width), kind),
@@ -191,9 +202,10 @@
             dma((groups,)),
             dma((2, groups)),
             dma,
+            dma((3,)),
         ],
         compiler_params=pltpu.CompilerParams(
-            collective_id=0, has_side_effects=True, vmem_limit_bytes=48 * 1024 * 1024
+            collective_id=0, has_side_effects=True, vmem_limit_bytes=62 * 1024 * 1024
         ),
     )(orbital_irrep, slab_irrep, virtual_count, amplitudes, integrals)
 

time: 40.4 us -> 32.7 us (0.81)
  the two profiles are of different devices: /device:TPU:0 before, /device:TPU:9 now
where the time goes in v2:
time: 32.7 us; the launch traced here: 32.6 us
  Pallas kernels  30.3 us (93%)
  local copies, waits for them, and re-layouts  2.26 us (7%)
    pallas_call x1, Pallas kernels, per_device(): pl.pallas_call(functools.partial(kernel, count), out_shape=jax.ShapeDtype...  30.3 us
    unnamed x1, local copies, waits for them, and re-layouts  2.26 us

profile of v2, /device:TPU:9, one launch (start us, length us, event | category | flops | bytes accessed | tf_op | source)
XLA Modules:
  0.0 32.6 jit_solution(1028927093304892647)
XLA Ops:
  0.0 30.3 %shard_map.55 = bf16[8,1,256,256]{3,2,1,0:T(8,128)(2,1)} custom-call(s32[8]{0:T(128)} %label_hbm.1, s32[4]{0:T(128)} %slab_hbm.1, s32[8]{0:T(128)} %size_hbm.1, bf16[1,1,2048,256]{3,2,1,0:T(8,128)(2,1)} %amp_ref.1, bf16[1,2048,2,256]{3,2,1,0:T(2,128)(2,1)} %int_ref.1), custom_call_target="tpu_custom_call" | custom-call | tf_op jit(solution)/shard_map/pallas_call | solution.py:181
  30.3 2.3 %copy.7 = bf16[8,1,256,256]{3,2,1,0:T(8,128)(2,1)} copy(bf16[8,1,256,256]{3,2,1,0:T(8,128)(2,1)} %shard_map.55) | data formatting | bytes 2097152

commit v3 on v2

v3 whole, which is shorter than its diff:
```python
import functools

import jax
import jax.numpy as jnp
from jax import lax
from jax.experimental import pallas as pl
from jax.experimental.pallas import tpu as pltpu
from jax.sharding import PartitionSpec as P

MESH = pl.DeviceIdType.MESH


def partner_of(me, step, count, back=False):
    if count & (count - 1):
        return (me + (count - step if back else step)) % count
    place, bit = 0, 1
    while bit < count:
        place = place + (((me // bit) % 2 + (step // bit) % 2) % 2) * bit
        bit *= 2
    return place


def each(low, high, body):
    if high - low <= 16:
        for step in range(low, high):
            body(step)
    else:
        lax.fori_loop(low, high, lambda step, carry: (body(step), carry)[1], 0)


def kernel(
    count,
    label_hbm, slab_hbm, size_hbm, amp_ref, int_ref, out_ref,
    label_ref, slab_ref, size_ref, landed, shared, staged, raw, own_tiles, sent_tiles, other_tiles,
    send_sem, land_sem, pass_sem, share_sem, done_sem, own_sem, raw_sem, tile_sem, label_sem,
):
    me = lax.axis_index("row")
    col = lax.axis_index("col")
    sibling = 1 - col
    rows, width = landed.shape[1:]
    groups = own_tiles.shape[0]
    near, late = count // 2, count - count // 4

    def target(step):
        return partner_of(me, step, count)

    def source(step):
        return partner_of(me, step, count, back=True)

    def block_of(there):
        return amp_ref.at[0, 0, pl.ds(pl.multiple_of(there * rows, rows), rows)]

    raw_copies = [
        pltpu.make_async_copy(
            int_ref.at[0, pl.ds(e * width, width)], raw.at[e], raw_sem.at[e]
        )
        for e in range(groups)
    ]
    label_copies = [
        pltpu.make_async_copy(origin, place, label_sem.at[number])
        for number, (origin, place) in enumerate(
            [(label_hbm, label_ref), (slab_hbm, slab_ref), (size_hbm, size_ref)]
        )
    ]

    def own_copy(step):
        slot = source(step)
        return pltpu.make_async_copy(block_of(target(step)), landed.at[slot], own_sem.at[step])

    def spread_copy(step):
        there = target(step)
        return pltpu.make_async_remote_copy(
            src_ref=block_of(there),
            dst_ref=landed.at[me],
            send_sem=send_sem.at[step],
            recv_sem=land_sem.at[step],
            device_id={"row": there},
            device_id_type=MESH,
        )

    def share_copy(step, local):
        slot = source(step)
        return pltpu.make_async_remote_copy(
            src_ref=block_of(target(step)) if local else landed.at[slot],
            dst_ref=shared.at[slot],
            send_sem=pass_sem.at[step],
            recv_sem=share_sem.at[step],
            device_id={"col": sibling},
            device_id_type=MESH,
        )

    def done_copy(step):
        return pltpu.make_async_remote_copy(
            src_ref=staged.at[step - late],
            dst_ref=out_ref.at[me, 0],
            send_sem=send_sem.at[step],
            recv_sem=done_sem.at[step - late],
            device_id={"row": target(step)},
            device_id_type=MESH,
        )

    for copy in label_copies + raw_copies:
        copy.start()
    each(late, count, lambda step: own_copy(step).start())
    own_copy(0).start()

    barrier = pltpu.get_barrier_semaphore()

    def greet(step):
        pl.semaphore_signal(
            barrier, inc=1, device_id={"row": target(step)}, device_id_type=MESH
        )

    each(1, count, greet)
    pl.semaphore_signal(barrier, inc=1, device_id={"col": sibling}, device_id_type=MESH)
    pl.semaphore_wait(barrier, count)

    each(near, late, lambda step: spread_copy(step).start())
    each(1, near, lambda step: spread_copy(step).start())
    each(late, count, lambda step: share_copy(step, True).start())
    share_copy(0, True).start()
    for copy in label_copies:
        copy.wait()

    own_label = slab_ref[col]
    other_label = slab_ref[sibling]
    place = lax.broadcasted_iota(jnp.int32, (width, width), 0)
    column = lax.broadcasted_iota(jnp.int32, (width, width), 1)

    def keep(tile, e, j):
        outer = size_ref[e ^ own_label ^ slab_ref[2 + j]]
        return jnp.where((place < size_ref[e]) & (column < outer), tile, jnp.zeros((), tile.dtype))

    tile_copies = []
    for e in range(groups):
        raw_copies[e].wait()
        tile_pair = raw[e]
        first = tile_pair[:, 0, :]
        second = tile_pair[:, 1, :]
        mine = jnp.where(col == 0, first, second)
        other = jnp.where(col == 0, second, first)
        sent_tiles[e] = keep(other, e, sibling)
        copy = pltpu.make_async_remote_copy(
            src_ref=sent_tiles.at[e],
            dst_ref=other_tiles.at[e],
            send_sem=tile_sem.at[0, e],
            recv_sem=tile_sem.at[1, e],
            device_id={"col": sibling},
            device_id_type=MESH,
        )
        copy.start()
        tile_copies.append(copy)
        own_tiles[e] = keep(mine, e, col)
    for copy in tile_copies:
        copy.wait_recv()

    row_place = lax.broadcasted_iota(jnp.int32, (rows, width), 0)

    def product(slot, there, orbital):
        first_virtual = there * rows
        group = first_virtual // width
        label = group ^ label_ref[orbital]
        total = jnp.dot(
            landed[slot], own_tiles[label ^ own_label], preferred_element_type=jnp.float32
        )
        total = total + jnp.dot(
            shared[slot], other_tiles[label ^ other_label], preferred_element_type=jnp.float32
        )
        real = row_place + first_virtual % width < size_ref[group]
        return jnp.where(real, total, 0.0).astype(out_ref.dtype)

    def depart(step):
        own_copy(step).wait()
        share_copy(step, True).wait_recv()
        staged[step - late] = product(source(step), target(step), me)
        done_copy(step).start()

    each(late, count, depart)

    def finish(step):
        share_copy(step, False).wait_recv()
        out_ref[source(step), 0] = product(source(step), me, source(step))

    own_copy(0).wait()
    finish(0)

    def arrive(step):
        spread_copy(step).wait_recv()
        share_copy(step, False).start()

    def arrive_then_finish(step):
        arrive(step)
        finish(step - 1)

    arrive(1)
    each(2, near, arrive_then_finish)
    each(near, late, arrive_then_finish)
    finish(late - 1)

    for copy in tile_copies:
        copy.wait_send()
    each(1, late, lambda step: spread_copy(step).wait_send())
    each(late, count, lambda step: done_copy(step).wait_send())
    each(1, late, lambda step: share_copy(step, False).wait_send())
    each(late, count, lambda step: share_copy(step, True).wait_send())
    share_copy(0, True).wait_send()
    each(late, count, lambda step: done_copy(step).wait_recv())


def per_device(amplitudes, integrals, orbital_irrep, slab_irrep, virtual_count, count):
    virtual_total, width = amplitudes.shape[2:]
    groups = virtual_count.shape[0]
    rows = virtual_total // count
    late_count = count // 4
    kind = amplitudes.dtype
    dma = pltpu.SemaphoreType.DMA
    return pl.pallas_call(
        functools.partial(kernel, count),
        out_shape=pltpu.VMEM((count, 1, rows, width), kind),
        in_specs=[pl.BlockSpec(memory_space=pltpu.HBM)] * 5,
        out_specs=pl.BlockSpec(memory_space=pltpu.VMEM),
        scratch_shapes=[
            pltpu.SMEM(orbital_irrep.shape, jnp.int32),
            pltpu.SMEM(slab_irrep.shape, jnp.int32),
            pltpu.SMEM(virtual_count.shape, jnp.int32),
            pltpu.VMEM((count, rows, width), kind),
            pltpu.VMEM((count, rows, width), kind),
            pltpu.VMEM((late_count, rows, width), kind),
            pltpu.VMEM((groups, width, 2, width), kind),
            pltpu.VMEM((groups, width, width), kind),
            pltpu.VMEM((groups, width, width), kind),
            pltpu.VMEM((groups, width, width), kind),
            dma((count,)),
            dma((count,)),
            dma((count,)),
            dma((count,)),
            dma((late_count,)),
            dma((count,)),
            dma((groups,)),
            dma((2, groups)),
            dma((3,)),
        ],
        compiler_params=pltpu.CompilerParams(
            collective_id=0, has_side_effects=True, vmem_limit_bytes=48 * 1024 * 1024
        ),
    )(
        *[
            pltpu.with_memory_space_constraint(operand, pltpu.HBM)
            for operand in (orbital_irrep, slab_irrep, virtual_count, amplitudes, integrals)
        ]
    )


def solution(mesh):
    in_specs = (
        P(("parts", "row"), "col", None, None),
        P(("parts", "col"), None, None, None),
        P("parts"),
        P("parts"),
        P("parts"),
    )
    return jax.shard_map(
        functools.partial(per_device, count=mesh.shape["row"]),
        mesh=mesh,
        in_specs=in_specs,
        out_specs=P("parts", "col", "row", None),
        check_vma=False,
    )
```

time: 32.7 us -> 29.1 us (0.89); the launches traced: 32.6 us -> 28.6 us
  Pallas kernels: 30.3 us -> 27.6 us
  local copies, waits for them, and re-layouts: 2.26 us -> 0.97 us
    pallas_call x1, Pallas kernels: 30.3 us -> 27.6 us  [per_device(): pl.pallas_call(functools.partial(kernel, count), out_shape=pltpu.VMEM((co...]
    unnamed x1, local copies, waits for them, and re-layouts: 2.26 us -> 0.97 us
where the time goes in v3:
time: 29.1 us; the launch traced here: 28.6 us
  Pallas kernels  27.6 us (95%)
  local copies, waits for them, and re-layouts  0.97 us (3%)
    pallas_call x1, Pallas kernels, per_device(): pl.pallas_call(functools.partial(kernel, count), out_shape=pltpu.VMEM((co...  27.6 us
    unnamed x1, local copies, waits for them, and re-layouts  0.97 us

profile of v3, /device:TPU:9, one launch (start us, length us, event | category | flops | bytes accessed | tf_op | source)
XLA Modules:
  0.0 28.6 jit_solution(16919641385296171787)
XLA Ops:
  0.0 27.6 %shard_map.55 = bf16[8,1,256,256]{3,2,1,0:T(8,128)(2,1)S(1)} custom-call(s32[8]{0:T(128)} %label_hbm.1, s32[4]{0:T(128)} %slab_hbm.1, s32[8]{0:T(128)} %size_hbm.1, bf16[1,1,2048,256]{3,2,1,0:T(8,128)(2,1)} %amp_ref.1, bf16[1,2048,2,256]{3,2,1,0:T(2,128)(2,1)} %int_ref.1), custom_call_target="tpu_custom_call" | custom-call | tf_op jit(solution)/shard_map/pallas_call | solution.py:217
  27.6 1.0 %copy.7 = bf16[8,1,256,256]{3,2,1,0:T(8,128)(2,1)} copy(bf16[8,1,256,256]{3,2,1,0:T(8,128)(2,1)S(1)} %shard_map.55) | data formatting | bytes 2097152

commit v4 on v3

--- a/solution.py
+++ b/solution.py
@@ -31,15 +31,18 @@
 def kernel(
     count,
     label_hbm, slab_hbm, size_hbm, amp_ref, int_ref, out_ref,
-    label_ref, slab_ref, size_ref, landed, shared, staged, raw, own_tiles, sent_tiles, other_tiles,
-    send_sem, land_sem, pass_sem, share_sem, done_sem, own_sem, raw_sem, tile_sem, label_sem,
+    label_ref, slab_ref, size_ref, landed, shared, late_own, late_shared, staged, raw, own_tiles, sent_tiles, other_tiles,
+    send_sem, land_sem, pass_sem, share_sem, late_sem, done_sem, own_sem, raw_sem, tile_sem, label_sem, ready_sem,
 ):
     me = lax.axis_index("row")
     col = lax.axis_index("col")
     sibling = 1 - col
     rows, width = landed.shape[1:]
     groups = own_tiles.shape[0]
-    near, late = count // 2, count - count // 4
+    quarter = count // 4
+    near, late = count // 2, count - quarter
+    last = me // late
+    odd = (me // quarter) % 2
 
     def target(step):
         return partner_of(me, step, count)
@@ -63,9 +66,25 @@
         )
     ]
 
-    def own_copy(step):
-        slot = source(step)
-        return pltpu.make_async_copy(block_of(target(step)), landed.at[slot], own_sem.at[step])
+    def late_step(slot):
+        return late + slot - quarter * odd
+
+    own_copy = pltpu.make_async_copy(block_of(me), landed.at[me], own_sem.at[quarter])
+
+    def late_copy(slot):
+        return pltpu.make_async_copy(
+            block_of(target(late_step(slot))), late_own.at[slot], own_sem.at[slot]
+        )
+
+    def late_share(slot):
+        return pltpu.make_async_remote_copy(
+            src_ref=block_of(target(late_step(slot))),
+            dst_ref=late_shared.at[slot],
+            send_sem=late_sem.at[0, slot],
+            recv_sem=late_sem.at[1, slot],
+            device_id={"col": sibling},
+            device_id_type=MESH,
+        )
 
     def spread_copy(step):
         there = target(step)
@@ -78,10 +97,10 @@
             device_id_type=MESH,
         )
 
-    def share_copy(step, local):
+    def share_copy(step):
         slot = source(step)
         return pltpu.make_async_remote_copy(
-            src_ref=block_of(target(step)) if local else landed.at[slot],
+            src_ref=landed.at[slot],
             dst_ref=shared.at[slot],
             send_sem=pass_sem.at[step],
             recv_sem=share_sem.at[step],
@@ -89,36 +108,60 @@
             device_id_type=MESH,
         )
 
-    def done_copy(step):
+    def done_copy(step, slot):
         return pltpu.make_async_remote_copy(
-            src_ref=staged.at[step - late],
+            src_ref=staged.at[slot],
             dst_ref=out_ref.at[me, 0],
             send_sem=send_sem.at[step],
-            recv_sem=done_sem.at[step - late],
+            recv_sem=done_sem.at[step - near],
             device_id={"row": target(step)},
             device_id_type=MESH,
         )
 
     for copy in label_copies + raw_copies:
         copy.start()
-    each(late, count, lambda step: own_copy(step).start())
-    own_copy(0).start()
+    each(0, quarter, lambda slot: late_copy(slot).start())
+    own_copy.start()
 
     barrier = pltpu.get_barrier_semaphore()
 
-    def greet(step):
+    def signal(semaphore, step):
         pl.semaphore_signal(
-            barrier, inc=1, device_id={"row": target(step)}, device_id_type=MESH
-        )
-
-    each(1, count, greet)
+            semaphore, inc=1, device_id={"row": target(step)}, device_id_type=MESH
+        )
+
+    each(1, quarter, lambda step: signal(barrier, step))
     pl.semaphore_signal(barrier, inc=1, device_id={"col": sibling}, device_id_type=MESH)
-    pl.semaphore_wait(barrier, count)
-
-    each(near, late, lambda step: spread_copy(step).start())
-    each(1, near, lambda step: spread_copy(step).start())
-    each(late, count, lambda step: share_copy(step, True).start())
-    share_copy(0, True).start()
+
+    @pl.when(last == 0)
+    def _():
+        each(quarter, count, lambda step: signal(barrier, step))
+
+    pl.semaphore_wait(barrier, count - quarter * (1 - last))
+
+    @pl.when(last == 1)
+    def _():
+        each(quarter, count, lambda step: signal(ready_sem, step))
+
+    def send_now(step):
+        @pl.when(last + 1 > target(step) // late)
+        def _():
+            spread_copy(step).start()
+
+    def send_when_ready(step):
+        @pl.when(last < target(step) // late)
+        def _():
+            spread_copy(step).start()
+
+    each(near, late, lambda step: spread_copy(step + quarter * odd).start())
+    each(1, near, send_now)
+
+    @pl.when(last == 0)
+    def _():
+        pl.semaphore_wait(ready_sem, quarter)
+
+    each(1, near, send_when_ready)
+    each(0, quarter, lambda slot: late_share(slot).start())
     for copy in label_copies:
         copy.wait()
 
@@ -156,62 +199,77 @@
 
     row_place = lax.broadcasted_iota(jnp.int32, (rows, width), 0)
 
-    def product(slot, there, orbital):
+    def product(mine, other, there, orbital):
         first_virtual = there * rows
         group = first_virtual // width
         label = group ^ label_ref[orbital]
         total = jnp.dot(
-            landed[slot], own_tiles[label ^ own_label], preferred_element_type=jnp.float32
+            mine, own_tiles[label ^ own_label], preferred_element_type=jnp.float32
         )
         total = total + jnp.dot(
-            shared[slot], other_tiles[label ^ other_label], preferred_element_type=jnp.float32
+            other, other_tiles[label ^ other_label], preferred_element_type=jnp.float32
         )
         real = row_place + first_virtual % width < size_ref[group]
         return jnp.where(real, total, 0.0).astype(out_ref.dtype)
 
-    def depart(step):
-        own_copy(step).wait()
-        share_copy(step, True).wait_recv()
-        staged[step - late] = product(source(step), target(step), me)
-        done_copy(step).start()
-
-    each(late, count, depart)
+    def depart(slot):
+        late_copy(slot).wait()
+        late_share(slot).wait_recv()
+        step = late_step(slot)
+        staged[slot] = product(late_own[slot], late_shared[slot], target(step), me)
+        done_copy(step, slot).start()
+
+    each(0, quarter, depart)
+
+    own_copy.wait()
+    share_copy(0).start()
 
     def finish(step):
-        share_copy(step, False).wait_recv()
-        out_ref[source(step), 0] = product(source(step), me, source(step))
-
-    own_copy(0).wait()
-    finish(0)
+        share_copy(step).wait_recv()
+        there = source(step)
+        out_ref[there, 0] = product(landed[there], shared[there], me, there)
 
     def arrive(step):
         spread_copy(step).wait_recv()
-        share_copy(step, False).start()
+        share_copy(step).start()
 
     def arrive_then_finish(step):
         arrive(step)
         finish(step - 1)
 
-    arrive(1)
-    each(2, near, arrive_then_finish)
-    each(near, late, arrive_then_finish)
-    finish(late - 1)
+    each(1, near, arrive_then_finish)
+
+    @pl.when(odd == 0)
+    def _():
+        each(near, count, arrive_then_finish)
+        finish(count - 1)
+
+    @pl.when(odd == 1)
+    def _():
+        finish(near - 1)
 
     for copy in tile_copies:
         copy.wait_send()
-    each(1, late, lambda step: spread_copy(step).wait_send())
-    each(late, count, lambda step: done_copy(step).wait_send())
-    each(1, late, lambda step: share_copy(step, False).wait_send())
-    each(late, count, lambda step: share_copy(step, True).wait_send())
-    share_copy(0, True).wait_send()
-    each(late, count, lambda step: done_copy(step).wait_recv())
+    each(1, near, lambda step: spread_copy(step).wait_send())
+    each(near, late, lambda step: spread_copy(step + quarter * odd).wait_send())
+    each(0, quarter, lambda slot: done_copy(late_step(slot), slot).wait_send())
+    each(0, quarter, lambda slot: late_share(slot).wait_send())
+    each(0, near, lambda step: share_copy(step).wait_send())
+
+    @pl.when(odd == 0)
+    def _():
+        each(near, count, lambda step: share_copy(step).wait_send())
+
+    @pl.when(odd == 1)
+    def _():
+        each(near, count, lambda step: done_copy(step, 0).wait_recv())
 
 
 def per_device(amplitudes, integrals, orbital_irrep, slab_irrep, virtual_count, count):
     virtual_total, width = amplitudes.shape[2:]
     groups = virtual_count.shape[0]
     rows = virtual_total // count
-    late_count = count // 4
+    quarter = count // 4
     kind = amplitudes.dtype
     dma = pltpu.SemaphoreType.DMA
     return pl.pallas_call(
@@ -225,7 +283,9 @@
             pltpu.SMEM(virtual_count.shape, jnp.int32),
             pltpu.VMEM((count, rows, width), kind),
             pltpu.VMEM((count, rows, width), kind),
-            pltpu.VMEM((late_count, rows, width), kind),
+            pltpu.VMEM((quarter, rows, width), kind),
+            pltpu.VMEM((quarter, rows, width), kind),
+            pltpu.VMEM((quarter, rows, width), kind),
             pltpu.VMEM((groups, width, 2, width), kind),
             pltpu.VMEM((groups, width, width), kind),
             pltpu.VMEM((groups, width, width), kind),
@@ -234,11 +294,13 @@
             dma((count,)),
             dma((count,)),
             dma((count,)),
-            dma((late_count,)),
-            dma((count,)),
+            dma((2, quarter)),
+            dma((count // 2,)),
+            dma((quarter + 1,)),
             dma((groups,)),
             dma((2, groups)),
             dma((3,)),
+            pltpu.SemaphoreType.REGULAR,
         ],
         compiler_params=pltpu.CompilerParams(
             collective_id=0, has_side_effects=True, vmem_limit_bytes=48 * 1024 * 1024

time: 29.1 us -> 28.8 us (0.990)
  no operation moved by 1% of the time
where the time goes in v4:
time: 28.8 us; the launch traced here: 28.4 us
  Pallas kernels  27.4 us (95%)
  local copies, waits for them, and re-layouts  0.97 us (3%)
    pallas_call x1, Pallas kernels, per_device(): pl.pallas_call(functools.partial(kernel, count), out_shape=pltpu.VMEM((co...  27.4 us
    unnamed x1, local copies, waits for them, and re-layouts  0.97 us

profile of v4, /device:TPU:9, one launch (start us, length us, event | category | flops | bytes accessed | tf_op | source)
XLA Modules:
  0.0 28.4 jit_solution(6955436613339508889)
XLA Ops:
  0.0 27.4 %shard_map.55 = bf16[8,1,256,256]{3,2,1,0:T(8,128)(2,1)S(1)} custom-call(s32[8]{0:T(128)} %label_hbm.1, s32[4]{0:T(128)} %slab_hbm.1, s32[8]{0:T(128)} %size_hbm.1, bf16[1,1,2048,256]{3,2,1,0:T(8,128)(2,1)} %amp_ref.1, bf16[1,2048,2,256]{3,2,1,0:T(2,128)(2,1)} %int_ref.1), custom_call_target="tpu_custom_call" | custom-call | tf_op jit(solution)/shard_map/pallas_call | solution.py:275
  27.4 1.0 %copy.7 = bf16[8,1,256,256]{3,2,1,0:T(8,128)(2,1)} copy(bf16[8,1,256,256]{3,2,1,0:T(8,128)(2,1)S(1)} %shard_map.55) | data formatting | bytes 2097152

commit v5 on v4

--- a/solution.py
+++ b/solution.py
@@ -219,7 +219,7 @@
         staged[slot] = product(late_own[slot], late_shared[slot], target(step), me)
         done_copy(step, slot).start()
 
-    each(0, quarter, depart)
+    each(0, quarter, lambda slot: depart(quarter - 1 - slot))
 
     own_copy.wait()
     share_copy(0).start()

time: 28.8 us -> 28.9 us (level)
  Pallas kernels: 27.4 us -> 27.8 us
    pallas_call x1, Pallas kernels: 27.4 us -> 27.8 us  [per_device(): pl.pallas_call(functools.partial(kernel, count), out_shape=pltpu.VMEM((co...]
where the time goes in v5:
time: 28.9 us; the launch traced here: 28.8 us
  Pallas kernels  27.8 us (96%)
  local copies, waits for them, and re-layouts  0.97 us (3%)
    pallas_call x1, Pallas kernels, per_device(): pl.pallas_call(functools.partial(kernel, count), out_shape=pltpu.VMEM((co...  27.8 us
    unnamed x1, local copies, waits for them, and re-layouts  0.97 us

profile of v5, /device:TPU:9, one launch (start us, length us, event | category | flops | bytes accessed | tf_op | source)
XLA Modules:
  0.0 28.8 jit_solution(5249667815682859386)
XLA Ops:
  0.0 27.8 %shard_map.55 = bf16[8,1,256,256]{3,2,1,0:T(8,128)(2,1)S(1)} custom-call(s32[8]{0:T(128)} %label_hbm.1, s32[4]{0:T(128)} %slab_hbm.1, s32[8]{0:T(128)} %size_hbm.1, bf16[1,1,2048,256]{3,2,1,0:T(8,128)(2,1)} %amp_ref.1, bf16[1,2048,2,256]{3,2,1,0:T(2,128)(2,1)} %int_ref.1), custom_call_target="tpu_custom_call" | custom-call | tf_op jit(solution)/shard_map/pallas_call | solution.py:275
  27.8 1.0 %copy.7 = bf16[8,1,256,256]{3,2,1,0:T(8,128)(2,1)} copy(bf16[8,1,256,256]{3,2,1,0:T(8,128)(2,1)S(1)} %shard_map.55) | data formatting | bytes 2097152
